TPU v7x, 32 devices: a whole 2x2x4 slice. The times are simulated.
32 devices in a mesh: parts: 2 (over y), rows: 16 (over z, x, core).
Axes of the slice: x: 2, y: 2, z: 4, core: 2. Of those that a mesh axis runs over, the one named last changes fastest.
Arguments:
- factor_panels: float32 [16384, 1536], P(('parts', 'rows')), parts along dimension 0, as said below
- targets: float32 [16384, 256], P(('parts', 'rows')), parts along dimension 0, may hold values from -6 to 6
- later_solutions: float32 [16384, 256], P(('parts', 'rows')), parts along dimension 0, as said below
Outputs:
- solved_rows: float32 [16384, 256], P(('parts', 'rows')), parts along dimension 0
There are 2 independent parts, one for each index of `parts`. A program takes and returns all parts, laid end to end along the dimension named above; each array names one. Nothing has to cross between parts.
Inputs may be any that keep to these rules, and one draw needn't show every extreme that they name: `factor_panels`: in rows of block d < 3, column blocks above d are zero and column block d holds a lower-triangular inverse diagonal block. `later_solutions`: the first 1536 rows are zero.
All inputs are finite; a program needn't handle non-finite values.
Results may differ from a plain program's by a relative error of at most 0.0001.
Values sent between devices are 32-bit elements; how exact they have to be, the bound alone decides.
A program may use at most 64 MiB of HBM per device.

v0:
```python
import jax
import jax.numpy as jnp
from jax import lax
from jax.sharding import PartitionSpec as P

exact_mode = lax.Precision.HIGHEST


def broadcast(shard, axis, root):
    mine = lax.axis_index(axis) == root
    return lax.psum(jnp.where(mine, shard, jnp.zeros_like(shard)), axis)


def product(left, right):
    return jnp.dot(left, right, precision=exact_mode, preferred_element_type=jnp.float32)


def transposed(left, right):
    return lax.dot_general(
        left,
        right,
        (((0,), (0,)), ((), ())),
        precision=exact_mode,
        preferred_element_type=jnp.float32,
    )


def local(factor_panels, targets, later_solutions):
    device = lax.axis_index("rows")
    block_rows = factor_panels.shape[0]
    panels = factor_panels.shape[1] // block_rows

    def panel_cols(panel):
        return factor_panels[:, panel * block_rows : (panel + 1) * block_rows]

    solved = []
    residual = targets
    for panel in range(panels):
        candidate = product(panel_cols(panel), residual)
        forward_part = broadcast(candidate, "rows", panel)
        solved.append(forward_part)
        residual = jnp.where(
            device > panel, residual - product(panel_cols(panel), forward_part), residual
        )
    answer = later_solutions
    for panel in reversed(range(panels)):
        partial_terms = jnp.where(device > panel, transposed(panel_cols(panel), answer), 0.0)
        fan_sum = lax.psum(partial_terms, "rows")
        candidate = transposed(panel_cols(panel), solved[panel] - fan_sum)
        answer = jnp.where(device == panel, candidate, answer)
    return jnp.where(device < panels, answer, residual)


def solution(mesh):
    in_specs = (P(("parts", "rows"), None), P(("parts", "rows"), None), P(("parts", "rows"), None))
    out_specs = P(("parts", "rows"), None)
    return jax.shard_map(local, mesh=mesh, in_specs=in_specs, out_specs=out_specs, check_vma=False)
```

profile of v0, /device:TPU:1, one launch (start us, length us, event | category | flops | bytes accessed | tf_op | source)
XLA Modules:
  0.0 503.3 jit_solution(16484655578196028900)
XLA Ops:
  6.5 0.0 copy-start
  6.5 0.0 all-reduce.7.cloned.1.call-start
  6.5 3.3 convolution_select_fusion.5
  9.8 0.0 all-reduce.7.cloned.1.call-update
  9.9 0.0 all-reduce.9.cloned.1.call-start
  9.9 93.7 %all-reduce.7.cloned.1.call-done = f32[512,256]{1,0:T(8,128)} async-done(((f32[512,256]{1,0:T(8,128)}), f32[512,256]{1,0:T(8,128)}) %all-reduce.7.cloned.1.call-update) | async-done | bytes 524304 | tf_op jit(solution)/shard_map/psum | solution.py:11
  103.6 2.5 fusion.13
  106.1 0.0 copy-start.5
  106.2 0.8 copy-done.5
  106.9 0.0 copy-done
  106.9 1.8 fusion.11
  108.7 0.0 all-reduce.9.cloned.1.call-update
  108.8 0.0 all-reduce.15.cloned.1.call-start
  108.8 3.7 convolution_select_fusion.2
  112.5 87.0 %all-reduce.9.cloned.1.call-done = f32[512,256]{1,0:T(8,128)} async-done(((f32[512,256]{1,0:T(8,128)}), f32[512,256]{1,0:T(8,128)}) %all-reduce.9.cloned.1.call-update) | async-done | bytes 524304 | tf_op jit(solution)/shard_map/psum | solution.py:11
  199.5 2.2 fusion.10
  201.7 0.0 copy-start.1
  201.7 0.8 copy-done.1
  202.5 1.8 fusion.8
  204.3 0.0 all-reduce.15.cloned.1.call-update
  204.3 0.0 all-reduce.11.cloned.1.call-start
  204.4 92.6 %all-reduce.15.cloned.1.call-done = (f32[512,256]{1,0:T(8,128)}, f32[512,256]{1,0:T(8,128)}) async-done(((f32[512,256]{1,0:T(8,128)}, f32[512,256]{1,0:T(8,128)}), (f32[512,256]{1,0:T(8,128)}, f32[512,256]{1,0:T(8,128)})) %all-reduce.15.cloned.1.call-update) | async-done | bytes 1048592 | tf_op jit(solution)/shard_map/psum | solution.py:11
  296.9 3.2 fusion.7
  300.1 0.0 copy-start.4
  300.1 0.8 copy-done.4
  300.9 2.6 fusion.6
  303.5 0.0 all-reduce.11.cloned.1.call-update
  303.6 0.2 all-reduce.13.cloned.1.call-start
  303.8 90.6 %all-reduce.11.cloned.1.call-done = f32[512,256]{1,0:T(8,128)} async-done(((f32[512,256]{1,0:T(8,128)}), f32[512,256]{1,0:T(8,128)}) %all-reduce.11.cloned.1.call-update) | async-done | bytes 524304 | tf_op jit(solution)/shard_map/psum | solution.py:48
  394.4 3.0 fusion.5
  397.4 0.0 copy-start.3
  397.4 0.8 copy-done.3
  398.2 2.6 fusion.4
  400.8 0.0 all-reduce.13.cloned.1.call-update
  400.9 90.8 %all-reduce.13.cloned.1.call-done = f32[512,256]{1,0:T(8,128)} async-done(((f32[512,256]{1,0:T(8,128)}), f32[512,256]{1,0:T(8,128)}) %all-reduce.13.cloned.1.call-update) | async-done | bytes 524304 | tf_op jit(solution)/shard_map/psum | solution.py:48
  491.7 0.0 copy-start.2
  491.7 0.0 copy-start.6
  491.7 3.3 fusion.3
  495.0 0.0 copy-done.2
  495.0 0.0 copy-done.6
  495.0 1.8 fusion.2
Async XLA Ops:
  6.5 100.4 %copy-start = (f32[512,1536]{1,0:T(8,128)S(1)}, f32[512,1536]{1,0:T(8,128)}, u32[]{:S(2)}) copy-start(f32[512,1536]{1,0:T(8,128)} %param.3) | copy-start | bytes 9437188
  6.5 97.1 %all-reduce.7.cloned.1.call-start = ((), (), s32[]{:S(2)}) async-start(), calls=%async_computation | async-start | bytes 1048576 | tf_op jit(solution)/shard_map/psum | solution.py:11
  9.9 189.6 %all-reduce.9.cloned.1.call-start = ((), (), s32[]{:S(2)}) async-start(), calls=%async_computation.1 | async-start | bytes 1048576 | tf_op jit(solution)/shard_map/psum | solution.py:11
  106.1 0.8 copy-start.5
  108.8 188.2 %all-reduce.15.cloned.1.call-start = ((), (), s32[]{:S(2)}) async-start(), calls=%async_computation.4 | async-start | bytes 2097152 | tf_op jit(solution)/shard_map/psum | solution.py:11
  201.7 0.8 copy-start.1
  204.3 190.1 %all-reduce.11.cloned.1.call-start = ((), (), s32[]{:S(2)}) async-start(), calls=%async_computation.2 | async-start | bytes 1048576 | tf_op jit(solution)/shard_map/psum | solution.py:48
  300.1 0.8 copy-start.4
  303.6 188.1 %all-reduce.13.cloned.1.call-start = ((), (), s32[]{:S(2)}) async-start(), calls=%async_computation.3 | async-start | bytes 1048576 | tf_op jit(solution)/shard_map/psum | solution.py:48
  397.4 0.8 copy-start.3
  491.7 3.3 copy-start.2
  491.7 3.3 copy-start.6
Sparse Core Ops, SparseCore 0:
  10.8 92.7 all-reduce.6
  108.9 90.5 all-reduce.8
  204.4 92.4 all-reduce.14
  303.7 90.6 all-reduce.10
  401.0 90.6 all-reduce.12
where the time goes:
time: 504 us; the launch traced here: 503 us
  waiting for transfers between devices  455 us (90%)
  matrix products  31.8 us (6%)
  between operations  13.3 us (3%)
    psum x3, waiting for transfers between devices, broadcast(): return lax.psum(jnp.where(mine, shard, jnp.zeros_like(shard)), axis)  273 us
    psum x2, waiting for transfers between devices, local(): fan_sum = lax.psum(partial_terms, 'rows')  181 us
    dot_general x6, matrix products, transposed(): lax.dot_general(left, right, (((0,), (0,)), ((), ())), precision=exact_mo...  18.3 us
    dot_general x6, matrix products, product(): jnp.dot(left, right, precision=exact_mode, preferred_element_type=jnp.flo...  13.5 us
  transfers between devices with their start and end apart: 5, of which 5 were waited for; matrix products, arithmetic and copies ran while one was open for 1% of the time, Pallas kernels for 0%

commit v1 on v0

--- a/solution.py
+++ b/solution.py
@@ -45,7 +45,8 @@
     answer = later_solutions
     for panel in reversed(range(panels)):
         partial_terms = jnp.where(device > panel, transposed(panel_cols(panel), answer), 0.0)
-        fan_sum = lax.psum(partial_terms, "rows")
+        parts = lax.all_gather(partial_terms, "rows")
+        fan_sum = jnp.sum(parts, axis=0)
         candidate = transposed(panel_cols(panel), solved[panel] - fan_sum)
         answer = jnp.where(device == panel, candidate, answer)
     return jnp.where(device < panels, answer, residual)

time: 504 us -> 579 us (1.15); the launches traced: 503 us -> 572 us
  waiting for transfers between devices: 455 us -> 485 us
  local copies, waits for them, and re-layouts: 3.15 us -> 29.4 us
  other arithmetic: 0 us -> 11.9 us
    all_gather x0 -> x3, waiting for transfers between devices: none -> 220 us  [local(): parts = lax.all_gather(partial_terms, 'rows')]
    psum x2 -> x0, waiting for transfers between devices: 181 us -> none  [local(): fan_sum = lax.psum(partial_terms, 'rows')]
    unnamed x14 -> x20, local copies, waits for them, and re-layouts: 3.15 us -> 25.3 us
    reduce_sum x0 -> x3, other arithmetic: none -> 11.9 us  [local(): fan_sum = jnp.sum(parts, axis=0)]
    psum x3, waiting for transfers between devices: 273 us -> 266 us  [broadcast(): return lax.psum(jnp.where(mine, shard, jnp.zeros_like(shard)), axis)]
  transfers between devices with their start and end apart: 5 -> 6, of which waited for: 5 -> 6; matrix products, arithmetic and copies ran while one was open for 1% -> 3% of each run, Pallas kernels for 0% -> 0%
where the time goes in v1:
time: 579 us; the launch traced here: 572 us
  waiting for transfers between devices  485 us (84%)
  matrix products  30.9 us (5%)
  local copies, waits for them, and re-layouts  29.4 us (5%)
  between operations  13.9 us (2%)
  other arithmetic  11.9 us (2%)
    psum x3, waiting for transfers between devices, broadcast(): return lax.psum(jnp.where(mine, shard, jnp.zeros_like(shard)), axis)  266 us
    all_gather x3, waiting for transfers between devices, local(): parts = lax.all_gather(partial_terms, 'rows')  220 us
    unnamed x20, local copies, waits for them, and re-layouts  25.3 us
    dot_general x6, matrix products, transposed(): lax.dot_general(left, right, (((0,), (0,)), ((), ())), precision=exact_mo...  15.6 us
    dot_general x6, matrix products, product(): jnp.dot(left, right, precision=exact_mode, preferred_element_type=jnp.flo...  15.2 us
    reduce_sum x3, other arithmetic, local(): fan_sum = jnp.sum(parts, axis=0)  11.9 us
  transfers between devices with their start and end apart: 6, of which 6 were waited for; matrix products, arithmetic and copies ran while one was open for 3% of the time, Pallas kernels for 0%

profile of v1, /device:TPU:1, one launch (start us, length us, event | category | flops | bytes accessed | tf_op | source)
XLA Modules:
  0.0 572.1 jit_solution(14324012116021466383)
XLA Ops:
  6.5 0.0 all-reduce.4.cloned.1.call-start
  6.5 3.3 convolution_select_fusion.5
  9.8 0.0 all-reduce.4.cloned.1.call-update
  9.9 0.0 all-reduce.6.cloned.1.call-start
  9.9 93.7 %all-reduce.4.cloned.1.call-done = f32[512,256]{1,0:T(8,128)} async-done(((f32[512,256]{1,0:T(8,128)}), f32[512,256]{1,0:T(8,128)}) %all-reduce.4.cloned.1.call-update) | async-done | bytes 524304 | tf_op jit(solution)/shard_map/psum | solution.py:11
  103.6 2.5 fusion.13
  106.1 0.0 copy-start.3
  106.2 0.8 copy-done.3
  106.9 0.0 copy-done
  106.9 2.7 fusion.11
  109.7 0.0 all-reduce.6.cloned.1.call-update
  109.7 0.0 all-gather.7.cloned.1.call-start
  109.7 3.7 convolution_select_fusion.2
  113.4 0.0 all-gather.7.cloned.1.call-update
  113.4 0.0 all-reduce.8.cloned.1.call-start
  113.5 86.9 %all-reduce.6.cloned.1.call-done = f32[512,256]{0,1:T(8,128)} async-done(((f32[512,256]{0,1:T(8,128)}), f32[512,256]{0,1:T(8,128)}) %all-reduce.6.cloned.1.call-update) | async-done | bytes 524304 | tf_op jit(solution)/shard_map/psum | solution.py:11
  200.4 2.2 fusion.10
  202.6 0.0 copy-start.1
  202.6 0.8 copy-done.1
  203.4 2.7 fusion.8
  206.1 0.0 all-reduce.8.cloned.1.call-update
  206.1 0.5 all-gather.9.cloned.1.call-start
  206.6 71.2 %all-gather.7.cloned.1.call-done = f32[8192,256]{1,0:T(8,128)} async-done(((f32[512,256]{1,0:T(8,128)}), f32[8192,256]{1,0:T(8,128)}) %all-gather.7.cloned.1.call-update) | async-done | bytes 8388624 | tf_op jit(solution)/shard_map/all_gather | solution.py:48
  277.8 4.8 reduce_sum.27
  282.6 2.0 copy.12
  284.6 85.0 %all-reduce.8.cloned.1.call-done = f32[512,256]{0,1:T(8,128)} async-done(((f32[512,256]{0,1:T(8,128)}), f32[512,256]{0,1:T(8,128)}) %all-reduce.8.cloned.1.call-update) | async-done | bytes 524304 | tf_op jit(solution)/shard_map/psum | solution.py:11
  369.6 3.2 fusion.7
  372.8 0.0 copy-start.5
  372.8 0.8 copy-done.5
  373.6 1.9 fusion.6
  375.4 0.0 all-gather.9.cloned.1.call-update
  375.5 0.0 all-gather.11.cloned.1.call-start
  375.5 75.3 %all-gather.9.cloned.1.call-done = f32[8192,256]{0,1:T(8,128)} async-done(((f32[512,256]{0,1:T(8,128)}), f32[8192,256]{0,1:T(8,128)}) %all-gather.9.cloned.1.call-update) | async-done | bytes 8388624 | tf_op jit(solution)/shard_map/all_gather | solution.py:48
  450.8 10.9 %copy.24 = f32[32,8,16,512]{3,2,1,0:T(8,128)S(1)} copy(f32[32,8,16,512]{3,1,2,0:T(8,128)} %bitcast.62) | data formatting | bytes 16777216
  461.8 0.0 copy-start.6
  461.8 0.0 copy-start.8
  461.8 3.3 bitcast_reduce_fusion.1
  465.1 1.8 fusion.5
  466.9 0.0 copy-start.4
  466.9 0.8 copy-done.4
  467.7 1.9 fusion.4
  469.6 0.0 all-gather.11.cloned.1.call-update
  469.6 73.3 %all-gather.11.cloned.1.call-done = f32[8192,256]{0,1:T(8,128)} async-done(((f32[512,256]{0,1:T(8,128)}), f32[8192,256]{0,1:T(8,128)}) %all-gather.11.cloned.1.call-update) | async-done | bytes 8388624 | tf_op jit(solution)/shard_map/all_gather | solution.py:48
  542.9 11.2 %copy.25 = f32[32,8,16,512]{3,2,1,0:T(8,128)S(1)} copy(f32[32,8,16,512]{3,1,2,0:T(8,128)} %bitcast.61) | data formatting | bytes 16777216
  554.1 3.8 bitcast_reduce_fusion
  557.9 2.0 copy.15
  559.9 3.3 fusion.3
  563.2 1.8 fusion.2
  (7 shorter events, 0.0 us)
Async XLA Ops:
  6.5 100.4 %copy-start = (f32[512,1536]{1,0:T(8,128)S(1)}, f32[512,1536]{1,0:T(8,128)}, u32[]{:S(2)}) copy-start(f32[512,1536]{1,0:T(8,128)} %param.3) | copy-start | bytes 9437188
  6.5 97.1 %all-reduce.4.cloned.1.call-start = ((), (), s32[]{:S(2)}) async-start(), calls=%async_computation | async-start | bytes 1048576 | tf_op jit(solution)/shard_map/psum | solution.py:11
  9.9 190.5 %all-reduce.6.cloned.1.call-start = ((), (), s32[]{:S(2)}) async-start(), calls=%async_computation.1 | async-start | bytes 1048576 | tf_op jit(solution)/shard_map/psum | solution.py:11
  106.1 0.8 copy-start.3
  109.7 168.1 %all-gather.7.cloned.1.call-start = ((), (), s32[]{:S(2)}) async-start(), calls=%async_computation.3 | async-start | bytes 8912896 | tf_op jit(solution)/shard_map/all_gather | solution.py:48
  113.4 256.2 %all-reduce.8.cloned.1.call-start = ((), (), s32[]{:S(2)}) async-start(), calls=%async_computation.2 | async-start | bytes 1048576 | tf_op jit(solution)/shard_map/psum | solution.py:11
  202.6 0.8 copy-start.1
  206.1 244.7 %all-gather.9.cloned.1.call-start = ((), (), s32[]{:S(2)}) async-start(), calls=%async_computation.4 | async-start | bytes 8912896 | tf_op jit(solution)/shard_map/all_gather | solution.py:48
  372.8 0.8 copy-start.5
  375.5 167.4 %all-gather.11.cloned.1.call-start = ((), (), s32[]{:S(2)}) async-start(), calls=%async_computation.5 | async-start | bytes 8912896 | tf_op jit(solution)/shard_map/all_gather | solution.py:48
  461.8 3.3 copy-start.6
  461.8 3.3 copy-start.8
  466.9 0.8 copy-start.4
  559.9 3.3 copy-start.2
  559.9 3.3 copy-start.7
Sparse Core Ops, SparseCore 0:
  10.8 92.7 all-reduce.3
  109.8 90.5 all-reduce.5
  202.5 75.1 all-gather.6
  281.0 88.5 all-reduce.7
  375.6 75.1 all-gather.8
  469.7 73.1 all-gather.10
